TPU v7x, 32 devices: a whole 2x2x4 slice. The times are simulated.
32 devices in a mesh: ctx: 8 (over z, y), tp: 4 (over x, core).
Axes of the slice: x: 2, y: 2, z: 4, core: 2. Of those that a mesh axis runs over, the one named last changes fastest.
Arguments:
- query_proj: bfloat16 [1024, 4096], P('ctx', 'tp'), may hold values from -6 to 6
- key_proj: bfloat16 [1024, 4096], P('ctx', 'tp'), may hold values from -6 to 6
- value_proj: bfloat16 [1024, 4096], P('ctx', 'tp'), may hold values from -6 to 6
- filters: float32 [256, 128], P('tp'), may hold values from -0.5 to 0.5
- skip_gain: float32 [4096], P('tp'), may hold values from -1 to 1
- out_grad: bfloat16 [1024, 4096], P('ctx', 'tp'), may hold values from -6 to 6
- w_out: bfloat16 [4096, 4096], P('tp'), may hold values from -0.09375 to 0.09375
Outputs:
- query_grad: bfloat16 [1024, 4096], P('ctx', 'tp')
- key_grad: bfloat16 [1024, 4096], P('ctx', 'tp')
- value_grad: bfloat16 [1024, 4096], P('ctx', 'tp')
- filter_grad: float32 [256, 128], P('tp')
- skip_grad: float32 [4096], P('tp')
All inputs are finite; a program needn't handle non-finite values.
Results may differ from a plain program's by a relative error of at most 0.0075.
Values may be sent and summed in bfloat16 or wider, within the bound.
A program may use at most 128 MiB of HBM per device.

v0:
```python
import jax
import jax.numpy as jnp
from jax import lax
from jax.sharding import PartitionSpec as P


def passed_along(block, axis, distance):
    devices = range(lax.axis_size(axis))
    route = [(i - distance, i) for i in devices if i - distance in devices]
    return lax.ppermute(block, axis, route)


def blocks_of(extended, width):
    count = (extended.shape[0] - width) // width
    channels = extended.shape[1]
    first = extended[:-width].reshape(count, width, channels)
    second = extended[width:].reshape(count, width, channels)
    return jnp.concatenate([first, second], axis=1)


def tap_table(filters, causal):
    width = filters.shape[1]
    rows = jnp.arange(width)[:, None]
    cols = jnp.arange(2 * width)[None, :]
    lag = rows + width - cols if causal else cols - rows
    valid = (lag >= 0) & (lag < width)
    index = jnp.clip(lag, 0, width - 1)
    table = filters[:, index]
    return jnp.where(valid[None], table, jnp.float32(0.0))


def convolve(extended, filters, skip_gain, causal):
    width = filters.shape[1]
    groups = filters.shape[0]
    channels = extended.shape[1]
    window = blocks_of(extended, width)
    count = window.shape[0]
    window = window.reshape(count, 2 * width, groups, channels // groups).astype(jnp.float32)
    mixed = jnp.einsum(
        "gij,bjgc->bigc", tap_table(filters, causal), window, precision=lax.Precision.HIGHEST
    )
    mixed = mixed.reshape(count * width, channels)
    current = extended[width:] if causal else extended[:-width]
    return mixed + skip_gain[None, :] * current.astype(jnp.float32)


def diagonal_lags(pairs, width):
    leading = pairs.shape[:-2]
    flat = pairs.reshape(leading + (width * 2 * width,))
    padded = jnp.concatenate([flat, jnp.zeros(leading + (width,), jnp.float32)], axis=-1)
    skewed = padded.reshape(leading + (width, 2 * width + 1)).sum(axis=-2)
    return skewed[..., width:0:-1]


def on_device(query_proj, key_proj, value_proj, filters, skip_gain, out_grad, w_out):
    width = filters.shape[1]
    groups = filters.shape[0]
    tok_rows = query_proj.shape[0]
    channels = query_proj.shape[1]
    span = channels // groups
    rim_rows = width - 1
    count = tok_rows // width
    query_f = query_proj.astype(jnp.float32)
    key_f = key_proj.astype(jnp.float32)
    value_f = value_proj.astype(jnp.float32)
    products = (key_f * value_f).astype(jnp.bfloat16)
    product_f = products.astype(jnp.float32)
    mixer_grad = lax.dot_general(
        lax.all_gather(out_grad, "tp", axis=1, tiled=True),
        w_out,
        (((1,), (1,)), ((), ())),
        preferred_element_type=jnp.float32,
    )
    earlier = passed_along(products[tok_rows - rim_rows :], "ctx", 1)
    single = jnp.zeros((1, channels), jnp.bfloat16)
    prod_ext = jnp.concatenate([single, earlier, products], axis=0)
    filtered = convolve(prod_ext, filters, skip_gain, True)
    query_grad = (mixer_grad * filtered).astype(jnp.bfloat16)
    filtered_grad = (mixer_grad * query_f).astype(jnp.bfloat16)
    grad_f = filtered_grad.astype(jnp.float32)
    later = passed_along(filtered_grad[:rim_rows], "ctx", -1)
    grad_ext = jnp.concatenate([filtered_grad, later, single], axis=0)
    product_grad = convolve(grad_ext, filters, skip_gain, False)
    key_grad = (product_grad * value_f).astype(jnp.bfloat16)
    value_grad = (product_grad * key_f).astype(jnp.bfloat16)
    window = blocks_of(prod_ext, width)
    grad_blocks = filtered_grad.reshape(count, width, channels)
    skip_part = jnp.sum(grad_f * product_f, axis=0)
    pairs = jnp.einsum(
        "bigc,bjgc->gij",
        grad_blocks.reshape(count, width, groups, span),
        window.reshape(count, 2 * width, groups, span),
        preferred_element_type=jnp.float32,
    )
    grouped = diagonal_lags(pairs, width)
    filter_grad, skip_grad = lax.psum((grouped, skip_part), "ctx")
    return (query_grad, key_grad, value_grad, filter_grad, skip_grad)


def solution(mesh):
    return jax.shard_map(
        on_device,
        mesh=mesh,
        in_specs=(
            P("ctx", "tp"),
            P("ctx", "tp"),
            P("ctx", "tp"),
            P("tp", None),
            P("tp"),
            P("ctx", "tp"),
            P("tp", None),
        ),
        out_specs=(P("ctx", "tp"), P("ctx", "tp"), P("ctx", "tp"), P("tp", None), P("tp")),
        check_vma=False,
    )
```

profile of v0, /device:TPU:0, one launch (start us, length us, event | category | flops | bytes accessed | tf_op | source)
XLA Modules:
  0.0 376.2 jit_solution(13880040861033989793)
XLA Ops:
  7.2 0.0 copy-start.2
  7.2 0.0 all-gather.2.cloned.1.call-start
  7.2 0.7 all-gather.2.cloned.1.call-update
  8.0 0.1 copy.37
  8.0 0.1 fusion.21
  8.1 0.1 copy.36
  8.3 20.7 %all-gather.2.cloned.1.call-done = bf16[128,4096]{1,0:T(8,128)(2,1)} async-done(((bf16[128,1024]{1,0:T(8,128)(2,1)}), bf16[128,4096]{1,0:T(8,128)(2,1)}) %all-gather.2.cloned.1.call-update) | async-done | bytes 1048592 | tf_op jit(solution)/shard_map/all_gather | solution.py:69
  29.0 6.7 %fusion.17 = (f32[1024]{0:T(1024)S(1)}, bf16[128,1024]{1,0:T(8,128)(2,1)S(1)}, bf16[128,1024]{1,0:T(8,128)(2,1)S(1)}, f32[128,1024]{1,0:T(8,128)S(1)}) fusion(bf16[128,1024]{1,0:T(8,128)(2,1)} %param.7, bf16[128,1024]{1,0:T(8,128)(2,1)} %param.9, bf16[128,1024]{1,0:T(8,128)(2,1)} %param.8, bf16[128,4096]{1,0:T(8,128)(2,1)} %all-gather.2.cloned.1.call-done, ...), kind=kOutput, calls=%fused_computation.25 | convolution fusion | flops 1075182592 | bytes 11276288 | tf_op jit(solution)/shard_map/dot_general | solution.py:68
  35.8 1.3 collective-permute-start.1
  37.1 0.0 copy-done.2
  37.1 0.1 copy.25
  37.2 108.4 %gather_fusion.1 = f32[32768,64]{1,0:T(8,128)} fusion(f32[64,128]{0,1:T(8,128)S(1)} %copy.25, s32[32768]{0:T(1024)S(1)} %broadcast_clamp_fusion), kind=kCustom, calls=%fused_computation.1 | custom fusion | bytes 16908288 | tf_op jit(solution)/shard_map/gather | solution.py:28
  145.6 13.6 %copy.31 = f32[128,256,64]{1,0,2:T(8,128)} copy(f32[128,256,64]{2,1,0:T(8,128)} %bitcast.45) | data formatting | bytes 16777216 | tf_op jit(solution)/shard_map/gather | solution.py:28
  159.2 108.3 %gather_fusion = f32[32768,64]{1,0:T(8,128)} fusion(f32[64,128]{0,1:T(8,128)S(1)} %copy.25, s32[32768]{0:T(1024)S(1)} %broadcast_clamp_fusion.1), kind=kCustom, calls=%fused_computation | custom fusion | bytes 16908288 | tf_op jit(solution)/shard_map/gather | solution.py:28
  267.5 13.6 %copy.26 = f32[128,256,64]{1,0,2:T(8,128)} copy(f32[128,256,64]{2,1,0:T(8,128)} %bitcast.44) | data formatting | bytes 16777216 | tf_op jit(solution)/shard_map/gather | solution.py:28
  281.1 0.1 fusion.27
  281.2 0.2 copy.28
  281.4 0.2 copy.24
  281.6 0.1 slice.19
  281.6 4.7 %collective-permute-start = (bf16[127,1024]{1,0:T(8,128)(2,1)S(1)}, bf16[127,1024]{1,0:T(8,128)(2,1)S(1)}, u32[]{:S(2)}, u32[]{:S(2)}) collective-permute-start(bf16[127,1024]{1,0:T(8,128)(2,1)S(1)} %slice.19), channel_id=1, source_target_pairs={{0,4},{4,8},{8,12},{12,16},{16,20},{20,24},{24,28},{1,5},{5,9},{9,... | collective-permute-start | bytes 780296 | tf_op jit(solution)/shard_map/ppermute | solution.py:10
  286.4 0.0 collective-permute-done.1
  286.4 0.2 copy.35
  286.6 0.1 concatenate.32.clone
  286.6 6.5 %fusion = f32[64,16,128]{2,1,0:T(8,128)S(1)} fusion(f32[128,256,64]{1,0,2:T(8,128)} %copy.31, pred[128,256]{1,0:T(8,128)(4,1)S(1)} %fusion.28, bf16[1,128,64,16]{1,3,2,0:T(8,128)(2,1)S(1)} %bitcast.57, bf16[1,128,64,16]{1,3,2,0:T(8,128)(2,1)S(1)} %bitcast.50), kind=kOutput, calls=%fused_computation.2 | convolution fusion | flops 405798912 | bytes 9469952 | tf_op jit(solution)/shard_map/gij,bjgc->bigc/dot_general | solution.py:39
  293.2 0.2 copy.32
  293.4 0.0 collective-permute-done
  293.4 0.2 copy.34
  293.6 0.1 concatenate.27.clone
  293.7 6.5 %fusion.2 = f32[64,16,128]{2,1,0:T(8,128)S(1)} fusion(f32[128,256,64]{1,0,2:T(8,128)} %copy.26, pred[128,256]{1,0:T(8,128)(4,1)S(1)} %fusion.27, bf16[1,128,64,16]{1,3,2,0:T(8,128)(2,1)S(1)} %bitcast.52, bf16[1,128,64,16]{1,3,2,0:T(8,128)(2,1)S(1)} %bitcast.48), kind=kOutput, calls=%fused_computation.4 | convolution fusion | flops 405798912 | bytes 9469952 | tf_op jit(solution)/shard_map/gij,bjgc->bigc/dot_general | solution.py:39
  300.3 0.2 copy.27
  300.5 1.3 fusion.20
  301.8 4.7 %copy.38 = f32[8,8,128,256]{3,1,2,0:T(8,128)S(1)} copy(f32[8,8,128,256]{3,2,1,0:T(8,128)S(1)} %bitcast.47) | data formatting | bytes 16777216
  306.5 3.8 concatenate.35
  310.3 14.2 %reshape.171 = f32[64,128,257]{2,1,0:T(8,128)} reshape(f32[64,32896]{1,0:T(8,128)} %concatenate.35) | data formatting | bytes 16842752 | tf_op jit(solution)/shard_map/reshape | solution.py:51
  324.4 0.0 copy-start
  324.4 0.0 copy-start.1
  324.4 0.0 copy-start.3
  324.4 6.1 %reduce_sum.18 = f32[64,257]{1,0:T(8,128)S(1)} reduce(f32[64,128,257]{2,1,0:T(8,128)} %reshape.171, f32[]{:T(128)} %constant.1.clone.1), dimensions={1}, to_apply=%region_0.1 | reduce | flops 2088896 | bytes 8487172 | tf_op jit(solution)/shard_map/reduce_sum | solution.py:51
  330.6 0.1 slice.21
  330.7 0.1 rev.3
  330.7 37.5 %all-reduce.3 = (f32[64,128]{1,0:T(8,128)}, f32[1024]{0:T(1024)}) all-reduce(f32[64,128]{1,0:T(8,128)S(1)} %rev.3, f32[1024]{0:T(1024)S(1)} %get-tuple-element.7), channel_id=1, replica_groups=mesh['ctx'=8,'tp'=4] {'ctx'}, use_global_device_ids=true, to_apply=%region_1.2 | all-reduce | flops 9216 | bytes 73728 | tf_op jit(solution)/shard_map/psum | solution.py:96
  368.2 0.0 copy-done
  368.2 0.0 copy-done.1
  368.3 0.0 copy-done.3
  368.3 1.1 fusion.10
  (5 shorter events, 0.1 us)
Async XLA Ops:
  7.2 29.9 %copy-start.2 = (f32[64,128]{1,0:T(8,128)S(1)}, f32[64,128]{1,0:T(8,128)}, u32[]{:S(2)}) copy-start(f32[64,128]{1,0:T(8,128)} %param.10) | copy-start | bytes 98308
  7.2 21.9 %all-gather.2.cloned.1.call-start = ((), (), s32[]{:S(2)}) async-start(), calls=%async_computation | async-start | bytes 1310720 | tf_op jit(solution)/shard_map/all_gather | solution.py:69
  35.8 250.6 %collective-permute-start.1 = (bf16[127,1024]{1,0:T(8,128)(2,1)S(1)}, bf16[127,1024]{1,0:T(8,128)(2,1)S(1)}, u32[]{:S(2)}, u32[]{:S(2)}) collective-permute-start(bf16[127,1024]{1,0:T(8,128)(2,1)S(1)} %bitcast.54), channel_id=1, source_target_pairs={{4,0},{8,4},{12,8},{16,12},{20,16},{24,20},{28,24},{5,1},{9,5},{13... | collective-permute-start | bytes 780296 | tf_op jit(solution)/shard_map/ppermute | solution.py:10
  281.6 11.8 %collective-permute-start = (bf16[127,1024]{1,0:T(8,128)(2,1)S(1)}, bf16[127,1024]{1,0:T(8,128)(2,1)S(1)}, u32[]{:S(2)}, u32[]{:S(2)}) collective-permute-start(bf16[127,1024]{1,0:T(8,128)(2,1)S(1)} %slice.19), channel_id=1, source_target_pairs={{0,4},{4,8},{8,12},{12,16},{16,20},{20,24},{24,28},{1,5},{5,9},{9,... | collective-permute-start | bytes 780296 | tf_op jit(solution)/shard_map/ppermute | solution.py:10
  324.4 43.8 %copy-start = (bf16[128,1024]{1,0:T(8,128)(2,1)S(1)}, bf16[128,1024]{1,0:T(8,128)(2,1)}, u32[]{:S(2)}) copy-start(bf16[128,1024]{1,0:T(8,128)(2,1)} %param.8) | copy-start | bytes 786436
  324.4 43.8 %copy-start.1 = (bf16[128,1024]{1,0:T(8,128)(2,1)S(1)}, bf16[128,1024]{1,0:T(8,128)(2,1)}, u32[]{:S(2)}) copy-start(bf16[128,1024]{1,0:T(8,128)(2,1)} %param.9) | copy-start | bytes 786436
  324.4 43.8 %copy-start.3 = (f32[1024]{0:T(1024)S(1)}, f32[1024]{0:T(1024)}, u32[]{:S(2)}) copy-start(f32[1024]{0:T(1024)} %param.11) | copy-start | bytes 12292
Sparse Core Ops, SparseCore 0:
  9.6 19.4 all-gather.1
where the time goes:
time: 377 us; the launch traced here: 376 us
  local copies, waits for them, and re-layouts  268 us (71%)
  blocking collectives  37.5 us (10%)
  waiting for transfers between devices  21.4 us (6%)
  matrix products  21.1 us (6%)
  between operations  14.2 us (4%)
  other arithmetic  7.52 us (2%)
  starting transfers between devices  6.07 us (2%)
    gather x4, local copies, waits for them, and re-layouts, tap_table(): table = filters[:, index]  244 us
    psum x1, blocking collectives, on_device(): filter_grad, skip_grad = lax.psum((grouped, skip_part), 'ctx')  37.5 us
    all_gather x1, waiting for transfers between devices, on_device(): lax.all_gather(out_grad, 'tp', axis=1, tiled=True)  20.7 us
    reshape x1, local copies, waits for them, and re-layouts, diagonal_lags(): skewed = padded.reshape(leading + (width, 2 * width + 1)).sum(axis=-2)  14.2 us
    dot_general x2, matrix products, convolve(): jnp.einsum('gij,bjgc->bigc', tap_table(filters, causal), window, precisio...  13.1 us
  transfers between devices with their start and end apart: 3, of which 1 were waited for; matrix products, arithmetic and copies ran while one was open for 67% of the time, Pallas kernels for 0%

commit v1 on v0

--- a/solution.py
+++ b/solution.py
@@ -2,6 +2,27 @@
 import jax.numpy as jnp
 from jax import lax
 from jax.sharding import PartitionSpec as P
+
+
+def in_order(blocks, dim):
+    lengths = list(blocks.shape[1:])
+    lengths[dim] *= blocks.shape[0]
+    return jnp.moveaxis(blocks, 0, dim).reshape(lengths)
+
+
+def grow_blocks(x, axis):
+    size, here = (lax.axis_size(axis), lax.axis_index(axis))
+    tiles, apart = (x[None], 1)
+    while apart < size:
+        theirs = lax.ppermute(tiles, axis, [(i, i ^ apart) for i in range(size)])
+        low = here & apart == 0
+        tiles = jnp.concatenate([jnp.where(low, tiles, theirs), jnp.where(low, theirs, tiles)])
+        apart *= 2
+    return tiles
+
+
+def gather_by_bits(x, axis, dim):
+    return in_order(grow_blocks(x, axis), dim)
 
 
 def passed_along(block, axis, distance):
@@ -66,7 +87,7 @@
     products = (key_f * value_f).astype(jnp.bfloat16)
     product_f = products.astype(jnp.float32)
     mixer_grad = lax.dot_general(
-        lax.all_gather(out_grad, "tp", axis=1, tiled=True),
+        gather_by_bits(out_grad, "tp", 1),
         w_out,
         (((1,), (1,)), ((), ())),
         preferred_element_type=jnp.float32,

time: 377 us -> 360 us (0.955)
  between operations: 14.2 us -> 0.88 us
  waiting for transfers between devices: 21.4 us -> 13 us
    all_gather x1 -> x0, waiting for transfers between devices: 20.7 us -> none  [on_device(): lax.all_gather(out_grad, 'tp', axis=1, tiled=True)]
    ppermute x0 -> x2, waiting for transfers between devices: none -> 13 us  [grow_blocks(): theirs = lax.ppermute(tiles, axis, [(i, i ^ apart) for i in range(size)])]
  transfers between devices with their start and end apart: 3 -> 4, of which waited for: 1 -> 2; matrix products, arithmetic and copies ran while one was open for 67% -> 70% of each run, Pallas kernels for 0% -> 0%
where the time goes in v1:
time: 360 us
  local copies, waits for them, and re-layouts  271 us (75%)
  blocking collectives  37.1 us (10%)
  matrix products  20.8 us (6%)
  waiting for transfers between devices  13 us (4%)
  starting transfers between devices  9.48 us (3%)
  other arithmetic  7.78 us (2%)
    gather x4, local copies, waits for them, and re-layouts, tap_table(): table = filters[:, index]  245 us
    psum x1, blocking collectives, on_device(): filter_grad, skip_grad = lax.psum((grouped, skip_part), 'ctx')  37.1 us
    reshape x1, local copies, waits for them, and re-layouts, diagonal_lags(): skewed = padded.reshape(leading + (width, 2 * width + 1)).sum(axis=-2)  14.2 us
    dot_general x2, matrix products, convolve(): jnp.einsum('gij,bjgc->bigc', tap_table(filters, causal), window, precisio...  13.1 us
    ppermute x2, waiting for transfers between devices, grow_blocks(): theirs = lax.ppermute(tiles, axis, [(i, i ^ apart) for i in range(size)])  13 us
  transfers between devices with their start and end apart: 4, of which 2 were waited for; matrix products, arithmetic and copies ran while one was open for 70% of the time, Pallas kernels for 0%

profile of v1, /device:TPU:0, one launch (start us, length us, event | category | flops | bytes accessed | tf_op | source)
XLA Modules:
  0.0 359.8 jit_solution(4110098657804011617)
XLA Ops:
  0.6 1.1 copy.23
  1.8 0.5 collective-permute-start
  2.3 0.1 copy.38
  2.4 0.1 fusion.21
  2.5 0.1 copy.37
  2.6 0.8 collective-permute-done
  3.5 0.0 copy-start.2
  3.5 0.1 pad_maximum_fusion.1
  3.5 2.9 collective-permute-start.1
  6.5 12.2 %collective-permute-done.1 = bf16[2,128,1024]{1,2,0:T(8,128)(2,1)S(1)} collective-permute-done((bf16[2,128,1024]{1,2,0:T(8,128)(2,1)S(1)}, bf16[2,128,1024]{1,2,0:T(8,128)(2,1)S(1)}, u32[]{:S(2)}, u32[]{:S(2)}) %collective-permute-start.1) | collective-permute-done | bytes 524320 | tf_op jit(solution)/shard_map/ppermute | solution.py:17
  18.7 0.1 broadcast_select_fusion.1
  18.8 0.1 pad_maximum_fusion
  18.9 6.5 %fusion.17 = (f32[1024]{0:T(1024)S(1)}, bf16[128,1024]{1,0:T(8,128)(2,1)S(1)}, bf16[128,1024]{1,0:T(8,128)(2,1)S(1)}, f32[128,1024]{1,0:T(8,128)S(1)}) fusion(bf16[128,1024]{1,0:T(8,128)(2,1)} %param.7, bf16[128,1024]{1,0:T(8,128)(2,1)} %param.9, bf16[128,1024]{1,0:T(8,128)(2,1)} %param.8, bf16[128,4096]{0,1:T(8,128)(2,1)S(1)} %bitcast.54, ...), kind=kOutput, calls=%fused_computation.26 | convolution fusion | flops 1075182592 | bytes 11276288 | tf_op jit(solution)/shard_map/dot_general | solution.py:89
  25.4 1.3 collective-permute-start.3
  26.7 0.0 copy-done.2
  26.7 0.1 copy.26
  26.8 109.0 %gather_fusion.1 = f32[32768,64]{1,0:T(8,128)} fusion(f32[64,128]{0,1:T(8,128)S(1)} %copy.26, s32[32768]{0:T(1024)S(1)} %broadcast_clamp_fusion), kind=kCustom, calls=%fused_computation.1 | custom fusion | bytes 16908288 | tf_op jit(solution)/shard_map/gather | solution.py:49
  135.8 13.6 %copy.32 = f32[128,256,64]{1,0,2:T(8,128)} copy(f32[128,256,64]{2,1,0:T(8,128)} %bitcast.51) | data formatting | bytes 16777216 | tf_op jit(solution)/shard_map/gather | solution.py:49
  149.4 109.0 %gather_fusion = f32[32768,64]{1,0:T(8,128)} fusion(f32[64,128]{0,1:T(8,128)S(1)} %copy.26, s32[32768]{0:T(1024)S(1)} %broadcast_clamp_fusion.1), kind=kCustom, calls=%fused_computation | custom fusion | bytes 16908288 | tf_op jit(solution)/shard_map/gather | solution.py:49
  258.4 13.6 %copy.27 = f32[128,256,64]{1,0,2:T(8,128)} copy(f32[128,256,64]{2,1,0:T(8,128)} %bitcast.50) | data formatting | bytes 16777216 | tf_op jit(solution)/shard_map/gather | solution.py:49
  272.0 0.1 fusion.27
  272.1 0.2 copy.29
  272.2 0.2 copy.25
  272.4 0.1 slice.19
  272.5 4.7 %collective-permute-start.2 = (bf16[127,1024]{1,0:T(8,128)(2,1)S(1)}, bf16[127,1024]{1,0:T(8,128)(2,1)S(1)}, u32[]{:S(2)}, u32[]{:S(2)}) collective-permute-start(bf16[127,1024]{1,0:T(8,128)(2,1)S(1)} %slice.19), channel_id=1, source_target_pairs={{0,4},{4,8},{8,12},{12,16},{16,20},{20,24},{24,28},{1,5},{5,9},{9,... | collective-permute-start | bytes 780296 | tf_op jit(solution)/shard_map/ppermute | solution.py:31
  277.3 0.0 collective-permute-done.3
  277.3 0.2 copy.36
  277.4 0.1 concatenate.40.clone
  277.5 6.5 %fusion = f32[64,16,128]{2,1,0:T(8,128)S(1)} fusion(f32[128,256,64]{1,0,2:T(8,128)} %copy.32, pred[128,256]{1,0:T(8,128)(4,1)S(1)} %fusion.28, bf16[1,128,64,16]{1,3,2,0:T(8,128)(2,1)S(1)} %bitcast.64, bf16[1,128,64,16]{1,3,2,0:T(8,128)(2,1)S(1)} %bitcast.57), kind=kOutput, calls=%fused_computation.2 | convolution fusion | flops 405798912 | bytes 9469952 | tf_op jit(solution)/shard_map/gij,bjgc->bigc/dot_general | solution.py:60
  284.0 0.2 copy.33
  284.3 0.0 collective-permute-done.2
  284.3 0.2 copy.35
  284.5 0.1 concatenate.35.clone
  284.6 6.5 %fusion.2 = f32[64,16,128]{2,1,0:T(8,128)S(1)} fusion(f32[128,256,64]{1,0,2:T(8,128)} %copy.27, pred[128,256]{1,0:T(8,128)(4,1)S(1)} %fusion.27, bf16[1,128,64,16]{1,3,2,0:T(8,128)(2,1)S(1)} %bitcast.59, bf16[1,128,64,16]{1,3,2,0:T(8,128)(2,1)S(1)} %bitcast.55), kind=kOutput, calls=%fused_computation.4 | convolution fusion | flops 405798912 | bytes 9469952 | tf_op jit(solution)/shard_map/gij,bjgc->bigc/dot_general | solution.py:60
  291.1 0.2 copy.28
  291.3 1.3 fusion.20
  292.6 4.7 %copy.39 = f32[8,8,128,256]{3,1,2,0:T(8,128)S(1)} copy(f32[8,8,128,256]{3,2,1,0:T(8,128)S(1)} %bitcast.53) | data formatting | bytes 16777216
  297.4 3.7 %concatenate.43 = f32[64,32896]{1,0:T(8,128)} pad(f32[64,32768]{1,0:T(8,128)S(1)} %bitcast.52, f32[]{:T(128)} %constant.4.clone.1), padding=0_0x0_128 | pad | bytes 16809988 | tf_op jit(solution)/shard_map/concatenate | solution.py:71
  301.1 14.2 %reshape.175 = f32[64,128,257]{2,1,0:T(8,128)} reshape(f32[64,32896]{1,0:T(8,128)} %concatenate.43) | data formatting | bytes 16842752 | tf_op jit(solution)/shard_map/reshape | solution.py:72
  315.3 0.0 copy-start
  315.3 6.1 %reduce_sum.18 = f32[64,257]{1,0:T(8,128)S(1)} reduce(f32[64,128,257]{2,1,0:T(8,128)} %reshape.175, f32[]{:T(128)} %constant.4.clone.1), dimensions={1}, to_apply=%region_0.1 | reduce | flops 2088896 | bytes 8487172 | tf_op jit(solution)/shard_map/reduce_sum | solution.py:72
  321.4 0.1 slice.21
  321.5 0.1 rev.3
  321.6 37.1 %all-reduce.3 = (f32[64,128]{1,0:T(8,128)}, f32[1024]{0:T(1024)}) all-reduce(f32[64,128]{1,0:T(8,128)S(1)} %rev.3, f32[1024]{0:T(1024)S(1)} %get-tuple-element.7), channel_id=1, replica_groups=mesh['ctx'=8,'tp'=4] {'ctx'}, use_global_device_ids=true, to_apply=%region_1.2 | all-reduce | flops 9216 | bytes 73728 | tf_op jit(solution)/shard_map/psum | solution.py:117
  358.7 0.0 copy-done
  358.7 0.0 copy-done.1
  358.7 0.0 copy-done.3
  358.7 1.1 fusion.10
  (8 shorter events, 0.2 us)
Async XLA Ops:
  1.8 1.7 collective-permute-start
  3.5 23.2 %copy-start.2 = (f32[64,128]{1,0:T(8,128)S(1)}, f32[64,128]{1,0:T(8,128)}, u32[]{:S(2)}) copy-start(f32[64,128]{1,0:T(8,128)} %param.10) | copy-start | bytes 98308
  3.5 15.2 %collective-permute-start.1 = (bf16[2,128,1024]{1,2,0:T(8,128)(2,1)S(1)}, bf16[2,128,1024]{1,2,0:T(8,128)(2,1)S(1)}, u32[]{:S(2)}, u32[]{:S(2)}) collective-permute-start(bf16[2,128,1024]{1,2,0:T(8,128)(2,1)S(1)} %pad_maximum_fusion.1), channel_id=1, source_target_pairs={{0,2},{1,3},{2,0},{3,1},{4,6},{5,7},{6,4},{7,5},{8,10},{9,11},{10,... | collective-permute-start | bytes 1572872 | tf_op jit(solution)/shard_map/ppermute | solution.py:17
  25.4 251.9 %collective-permute-start.3 = (bf16[127,1024]{1,0:T(8,128)(2,1)S(1)}, bf16[127,1024]{1,0:T(8,128)(2,1)S(1)}, u32[]{:S(2)}, u32[]{:S(2)}) collective-permute-start(bf16[127,1024]{1,0:T(8,128)(2,1)S(1)} %bitcast.61), channel_id=1, source_target_pairs={{4,0},{8,4},{12,8},{16,12},{20,16},{24,20},{28,24},{5,1},{9,5},{13... | collective-permute-start | bytes 780296 | tf_op jit(solution)/shard_map/ppermute | solution.py:31
  272.5 11.8 %collective-permute-start.2 = (bf16[127,1024]{1,0:T(8,128)(2,1)S(1)}, bf16[127,1024]{1,0:T(8,128)(2,1)S(1)}, u32[]{:S(2)}, u32[]{:S(2)}) collective-permute-start(bf16[127,1024]{1,0:T(8,128)(2,1)S(1)} %slice.19), channel_id=1, source_target_pairs={{0,4},{4,8},{8,12},{12,16},{16,20},{20,24},{24,28},{1,5},{5,9},{9,... | collective-permute-start | bytes 780296 | tf_op jit(solution)/shard_map/ppermute | solution.py:31
  315.3 43.4 %copy-start = (bf16[128,1024]{1,0:T(8,128)(2,1)S(1)}, bf16[128,1024]{1,0:T(8,128)(2,1)}, u32[]{:S(2)}) copy-start(bf16[128,1024]{1,0:T(8,128)(2,1)} %param.8) | copy-start | bytes 786436
  315.3 43.4 %copy-start.1 = (bf16[128,1024]{1,0:T(8,128)(2,1)S(1)}, bf16[128,1024]{1,0:T(8,128)(2,1)}, u32[]{:S(2)}) copy-start(bf16[128,1024]{1,0:T(8,128)(2,1)} %param.9) | copy-start | bytes 786436
  315.3 43.4 %copy-start.3 = (f32[1024]{0:T(1024)S(1)}, f32[1024]{0:T(1024)}, u32[]{:S(2)}) copy-start(f32[1024]{0:T(1024)} %param.11) | copy-start | bytes 12292
